TPU v7x, 32 devices: a whole 2x2x4 slice. The times are simulated.
32 devices in a mesh: img: 4 (over y, core), ref: 8 (over z, x).
Axes of the slice: x: 2, y: 2, z: 4, core: 2. Of those that a mesh axis runs over, the one named last changes fastest.
Arguments:
- images: float32 [2, 64, 32768], P(None, 'img', 'ref'), may hold values from -6 to 6
- references: float32 [2, 64, 32768], P(None, 'ref', 'img'), may hold values from -2 to 2
- precision: float32 [64], P('img'), may hold values from 0.00390625 to 0.0390625
- shifts: int32 [12, 2], replicated, may hold values from -6 to 6, as said below
- labels: int32 [64], P('ref'), may hold values from 0 to 3
- log_prior: float32 [4], replicated, may hold values from -4 to 4
Outputs:
- new_refs: float32 [2, 64, 32768], P(None, 'ref', 'img')
- class_post: float32 [64, 4], P('img')
Inputs may be any that keep to these rules, and one draw needn't show every extreme that they name: `shifts`: both ends of the range occur in every draw.
All inputs are finite; a program needn't handle non-finite values.
Results may differ from a plain program's by a relative error of at most 0.0056.
Values may be sent and summed in bfloat16 or wider, within the bound.
A program may use at most 64 MiB of HBM per device.

v0:
```python
import functools
import math

import jax
import jax.numpy as jnp
from jax import lax
from jax.experimental import pallas as pl
from jax.experimental.pallas import tpu as pltpu
from jax.sharding import PartitionSpec as P

ROWS = 256
COLS = 128
SHIFTS = 12
CLASSES = 4


def phases(shifts):
    index = jnp.arange(ROWS * COLS, dtype=jnp.int32)
    freq_y = (index // COLS - ROWS // 2).astype(jnp.float32)
    freq_x = (index % COLS).astype(jnp.float32)
    shift_x = shifts[:, 0].astype(jnp.float32)[:, None]
    shift_y = shifts[:, 1].astype(jnp.float32)[:, None]
    angles = 2.0 * math.pi / ROWS * (freq_x[None, :] * shift_x + freq_y[None, :] * shift_y)
    return (jnp.cos(angles), jnp.sin(angles))


def inner_rows(left, right):
    return lax.dot_general(
        left, right, (((1,), (1,)), ((), ())), preferred_element_type=jnp.float32
    )


def inner_cols(left, right):
    return lax.dot_general(
        left, right, (((0,), (0,)), ((), ())), preferred_element_type=jnp.float32
    )


def gathered(images, references, precision, shifts, labels, log_prior):
    img_low = lax.all_gather(images.astype(jnp.bfloat16), "ref", axis=2, tiled=True)
    ref_low = lax.all_gather(references.astype(jnp.bfloat16), "img", axis=2, tiled=True)
    pixels = img_low.shape[2]
    img_dev = img_low.shape[1]
    ref_dev = ref_low.shape[1]
    blocks = SHIFTS // 4
    cosine, sine_part = phases(shifts)
    cos_blocks = cosine.reshape(blocks, 4, pixels)
    sin_blocks = sine_part.reshape(blocks, 4, pixels)
    ref_wide = ref_low.astype(jnp.float32)
    energy = jnp.sum(ref_wide * ref_wide, axis=(0, 2))
    onehot = (labels[:, None] == jnp.arange(CLASSES, dtype=jnp.int32)[None, :]).astype(jnp.float32)
    prior_term = jnp.sum(onehot * log_prior[None, :], axis=1)

    def cross_block(operands):
        cos_rows, sin_rows = operands
        shifted_re = (
            ref_wide[0][None] * cos_rows[:, None, :] + ref_wide[1][None] * sin_rows[:, None, :]
        ).astype(jnp.bfloat16)
        shifted_im = (
            ref_wide[1][None] * cos_rows[:, None, :] - ref_wide[0][None] * sin_rows[:, None, :]
        ).astype(jnp.bfloat16)
        return inner_rows(img_low[0], shifted_re.reshape(4 * ref_dev, pixels)) + inner_rows(
            img_low[1], shifted_im.reshape(4 * ref_dev, pixels)
        )

    cross_terms = lax.map(cross_block, (cos_blocks, sin_blocks))
    cross_terms = jnp.transpose(cross_terms, (1, 0, 2)).reshape(img_dev, SHIFTS, ref_dev)
    scores = (
        precision[:, None, None] * (cross_terms - 0.5 * energy[None, None, :])
        + prior_term[None, None, :]
    )
    local_top = jnp.max(scores, axis=(1, 2))
    top_score = lax.pmax(local_top, "ref")
    exponent = jnp.exp(scores - top_score[:, None, None])
    local_class = jnp.einsum(
        "ik,kc->ic", jnp.sum(exponent, axis=1), onehot, precision=lax.Precision.HIGHEST
    )
    row_total, class_sum = lax.psum((jnp.sum(exponent, axis=(1, 2)), local_class), "ref")
    posterior = exponent / row_total[:, None, None]
    class_post = class_sum / row_total[:, None]
    local_mass = jnp.sum(posterior, axis=(0, 1))
    post_low = posterior.astype(jnp.bfloat16).reshape(img_dev, blocks, 4 * ref_dev)
    post_low = jnp.transpose(post_low, (1, 0, 2))

    def back_block(running, operands):
        weights_blk, cos_rows, sin_rows = operands
        back_re = inner_cols(weights_blk, img_low[0]).reshape(4, ref_dev, pixels)
        back_im = inner_cols(weights_blk, img_low[1]).reshape(4, ref_dev, pixels)
        part_re = jnp.sum(back_re * cos_rows[:, None, :] - back_im * sin_rows[:, None, :], axis=0)
        part_im = jnp.sum(back_im * cos_rows[:, None, :] + back_re * sin_rows[:, None, :], axis=0)
        return (running + jnp.stack([part_re, part_im]), None)

    start_sum = jnp.zeros((2, ref_dev, pixels), jnp.float32)
    summed, unused = lax.scan(back_block, start_sum, (post_low, cos_blocks, sin_blocks))
    summed_part = lax.psum_scatter(summed, "img", scatter_dimension=2, tiled=True)
    ref_mass = lax.psum(local_mass, "img")
    new_refs = summed_part / (ref_mass + 1.0)[None, :, None]
    return (new_refs, class_post)


MESH = pl.DeviceIdType.MESH
LANES = 128
CHUNK = 1024
OWNED = 2
PAIRS = SHIFTS // 2
TOGETHER = 4
GROUPS = SHIFTS // TOGETHER
STRIP = 512
CORES = 2
TURN_IN = False
TURN_OUT = True
REF_ROWS = 8


def exchange(src, dst, send_sem, recv_sem, img, ref):
    return pltpu.make_async_remote_copy(
        src_ref=src, dst_ref=dst, send_sem=send_sem, recv_sem=recv_sem, device_id=(img, ref), device_id_type=MESH
    )


def fused_kernel(
    n_img, n_ref,
    images_hbm, references_hbm, precision_hbm, shifts_hbm, labels_hbm, log_prior_hbm,
    new_refs, class_post,
    images, references, precision, shifts, labels, log_prior,
    img_send, img_buf, ref_send, ref_buf, cos_tab, sin_tab, rotated, shifted,
    energy_col, ref_mid, out_mid, part, part_in, own, own_in, post_buf, post_wide, out_send, out_buf, in_sem,
    img_ss, img_rs, ref_ss, ref_rs, part_ss, part_rs, own_ss, own_rs, post_ss, post_rs, out_ss, out_rs,
    ref_mid_ss, ref_mid_rs, out_mid_ss, out_mid_rs,
):
    n_dev = n_img * n_ref
    a = lax.axis_index("img")
    r = lax.axis_index("ref")
    me = a * n_ref + r
    per = n_ref // n_img
    img_dev = images.shape[1]
    n_images = n_img * img_dev
    n_refs = n_ref * REF_ROWS

    loads = [
        pltpu.make_async_copy(src, dst, in_sem.at[i])
        for i, (src, dst) in enumerate(
            (
                (references_hbm, references),
                (images_hbm, images),
                (shifts_hbm, shifts),
                (precision_hbm, precision),
                (labels_hbm, labels),
                (log_prior_hbm, log_prior),
            )
        )
    ]
    for load in loads:
        load.start()

    barrier = pltpu.get_barrier_semaphore()

    def greet(j, carry):
        other = lax.rem(me + j, n_dev)
        pl.semaphore_signal(barrier, inc=1, device_id=(other // n_ref, lax.rem(other, n_ref)), device_id_type=MESH)
        return carry

    lax.fori_loop(1, n_dev, greet, 0)

    loads[0].wait()
    for q in range(n_ref):
        px = pl.ds(q * CHUNK, CHUNK)
        both = jnp.concatenate([references[0, :, px], references[1, :, px]], axis=0)
        ref_send[q] = both.astype(jnp.bfloat16)

    pl.semaphore_wait(barrier, n_dev - 1)

    y, core = a // CORES, lax.rem(a, CORES)
    across = (1 - y) * CORES + core

    def ref_here(q):
        return (lax.rem(q, n_img) == a) & (per * a + q // n_img == r)

    def ref_by_way(q):
        if not TURN_IN:
            return jnp.bool_(False)
        at_mid = (lax.rem(q, n_img) == across) & (per * a + q // n_img == r)
        return (lax.rem(q, n_img) // CORES != y) & jnp.logical_not(at_mid)

    def ref_copy(q):
        return exchange(
            ref_send.at[q], ref_buf.at[r], ref_ss.at[q], ref_rs.at[r], lax.rem(q, n_img), per * a + q // n_img
        )

    def ref_hop(q):
        slot = (q // n_img) * CORES + lax.rem(q, CORES)
        return exchange(ref_send.at[q], ref_mid.at[slot], ref_ss.at[q], ref_mid_rs.at[slot], across, r)

    def ref_start(j, carry):
        q = lax.rem(me + j, n_ref)
        here = ref_here(q)
        by_way = ref_by_way(q)

        @pl.when(here)
        def _():
            ref_buf[r] = ref_send[q]

        @pl.when(by_way)
        def _():
            ref_hop(q).start()

        @pl.when(jnp.logical_not(here | by_way))
        def _():
            ref_copy(q).start()

        return carry

    lax.fori_loop(0, n_ref, ref_start, 0)

    def ref_forward(slot):
        to_img = y * CORES + slot % CORES
        to_ref = per * across + slot // CORES
        return (to_img == a) & (to_ref == r), exchange(
            ref_mid.at[slot], ref_buf.at[r], ref_mid_ss.at[slot], ref_rs.at[r], to_img, to_ref
        )

    loads[1].wait()
    for q in range(n_img):
        img_send[q] = images[:, :, q * CHUNK : (q + 1) * CHUNK].astype(jnp.bfloat16)
    img_buf[a] = img_send[a]
    img_copies = []
    for j in range(1, n_img):
        dest = lax.rem(a + j, n_img)
        copy = exchange(img_send.at[dest], img_buf.at[a], img_ss.at[j], img_rs.at[j], dest, r)
        copy.start()
        img_copies.append(copy)

    if TURN_IN:
        for slot in range(per * CORES):
            stays, copy = ref_forward(slot)

            @pl.when(jnp.logical_not(stays))
            def _():
                exchange(
                    ref_send.at[0], ref_mid.at[slot], ref_ss.at[0], ref_mid_rs.at[slot], across, r
                ).wait_recv()
                copy.start()

    row_first = r * (n_img * CHUNK // COLS) + a * (CHUNK // COLS) - ROWS // 2
    freq_y = lax.broadcasted_iota(jnp.int32, (CHUNK // COLS, COLS), 0) + row_first
    freq_x = lax.broadcasted_iota(jnp.int32, (CHUNK // COLS, COLS), 1)

    for load in loads[2:]:
        load.wait()
    for t in range(SHIFTS):
        turn = freq_x * shifts[0:1, t : t + 1] + freq_y * shifts[1:2, t : t + 1]
        turn = ((turn + ROWS // 2) & (ROWS - 1)) - ROWS // 2
        angle = turn.astype(jnp.float32) * (2.0 * math.pi / ROWS)
        cosine = jnp.cos(angle)
        sine = jnp.sin(angle)
        for n in range(CHUNK // COLS):
            px = slice(n * COLS, (n + 1) * COLS)
            cos_tab[t, :, px] = jnp.broadcast_to(cosine[n : n + 1], (8, COLS))
            sin_tab[t, :, px] = jnp.broadcast_to(sine[n : n + 1], (8, COLS))

    row = lax.broadcasted_iota(jnp.int32, (8, LANES), 0)
    lane = lax.broadcasted_iota(jnp.int32, (8, LANES), 1)
    label_row = jnp.concatenate([labels[...].astype(jnp.float32)] * (LANES // REF_ROWS), axis=1)
    label_row = jnp.where((lane // REF_ROWS) % n_ref == r, jnp.broadcast_to(label_row, (8, LANES)), 0.0)

    for copy in img_copies:
        copy.wait_recv()

    def rotate(t, carry):
        cos_row = cos_tab[t][None]
        sin_row = sin_tab[t][None]
        for b in range(n_img):
            re = img_buf[b, 0].astype(jnp.float32).reshape(img_dev // 8, 8, CHUNK)
            im = img_buf[b, 1].astype(jnp.float32).reshape(img_dev // 8, 8, CHUNK)
            rows = pl.ds(b * img_dev, img_dev)
            turned_re = (re * cos_row - im * sin_row).reshape(img_dev, CHUNK)
            turned_im = (im * cos_row + re * sin_row).reshape(img_dev, CHUNK)
            rotated[t, rows, 0:CHUNK] = turned_re.astype(jnp.bfloat16)
            rotated[t, rows, CHUNK : 2 * CHUNK] = turned_im.astype(jnp.bfloat16)
        return carry

    lax.fori_loop(0, SHIFTS, rotate, 0)

    def arrive(b):
        @pl.when(jnp.logical_not((a == r // per) & (b == r)))
        def _():
            exchange(ref_send.at[0], ref_buf.at[b], ref_ss.at[0], ref_rs.at[b], r // per, b).wait_recv()

    def shift(b, t):
        cos_row = cos_tab[t]
        sin_row = sin_tab[t]
        res = []
        ims = []
        for s in range(2):
            block = ref_buf[b + s].astype(jnp.float32)
            re = block[0:REF_ROWS]
            im = block[REF_ROWS : 2 * REF_ROWS]
            res.append(re * cos_row + im * sin_row)
            ims.append(im * cos_row - re * sin_row)
        rows = pl.ds(pl.multiple_of(b * REF_ROWS, 2 * REF_ROWS), 2 * REF_ROWS)
        shifted[t, rows, 0:CHUNK] = jnp.concatenate(res, axis=0).astype(jnp.bfloat16)
        shifted[t, rows, CHUNK : 2 * CHUNK] = jnp.concatenate(ims, axis=0).astype(jnp.bfloat16)

    def ready(b):
        arrive(b)
        arrive(b + 1)
        for s in range(2):
            block = ref_buf[b + s].astype(jnp.float32)
            square = jnp.sum(block * block, axis=1, keepdims=True)
            square = jnp.broadcast_to(square[0:REF_ROWS] + square[REF_ROWS : 2 * REF_ROWS], (REF_ROWS, LANES))
            energy_col[pl.ds(pl.multiple_of((b + s) * REF_ROWS, REF_ROWS), REF_ROWS)] = square

    layers = n_ref // 2

    def layer_step(i, carry):
        b = 2 * lax.rem(r // 2 + i, layers)
        ready(b)

        def turn_step(t, inner):
            shift(b, t)
            return inner

        return lax.fori_loop(0, SHIFTS, turn_step, carry)

    lax.fori_loop(0, layers - 1, layer_step, 0)
    last = 2 * lax.rem(r // 2 + layers - 1, layers)
    ready(last)
    energy = energy_col[...]
    half_energy = 0.5 * jnp.concatenate([energy, energy], axis=0).T[0:8][None]

    pictures = [img_buf[:, c].reshape(n_images, CHUNK) for c in range(2)]
    pictures = jnp.concatenate(pictures, axis=1)
    part_copies = []
    for g in range(GROUPS):
        for t in range(g * TOGETHER, (g + 1) * TOGETHER):
            shift(last, t)
        group = shifted[g * TOGETHER : (g + 1) * TOGETHER].reshape(TOGETHER * n_refs, 2 * CHUNK)
        cross = inner_rows(pictures, group)
        for h in range(TOGETHER // 2):
            pair = cross[:, h * LANES : (h + 1) * LANES]
            pair = (pair.reshape(n_images // 8, 8, LANES) - half_energy).reshape(n_img, img_dev, LANES)
            part[g, :, :, h * LANES : (h + 1) * LANES] = pair
        for j in range(1, n_img):
            dest = lax.rem(a + j, n_img)
            copy = exchange(
                part.at[g, dest], part_in.at[g, j - 1], part_ss.at[g, j], part_rs.at[g, j], dest, r
            )
            copy.start()
            part_copies.append(copy)

    own[...] = jnp.zeros_like(own)
    own[:, PAIRS, :] = jnp.broadcast_to(label_row[0:1], (img_dev, LANES))
    for copy in part_copies:
        copy.wait_recv()
    for g in range(GROUPS):
        total = part[g, a]
        for j in range(n_img - 1):
            total = total + part_in[g, j]
        for h in range(TOGETHER // 2):
            own[:, g * (TOGETHER // 2) + h, :] = total[:, h * LANES : (h + 1) * LANES]
    own_copies = []
    for j in range(1, n_ref):
        dest = lax.rem(r + j, n_ref)
        copy = exchange(own.at[pl.ds(OWNED * dest, OWNED)], own_in.at[j - 1], own_ss.at[j], own_rs.at[j], a, dest)
        copy.start()
        own_copies.append(copy)
    for copy in own_copies:
        copy.wait_recv()
    mine = own[pl.ds(OWNED * r, OWNED)]
    for j in range(n_ref - 1):
        mine = mine + own_in[j]
    label_lane = jnp.broadcast_to(mine[0, PAIRS : PAIRS + 1], (8, LANES))
    prior = jnp.zeros((8, LANES), jnp.float32)
    for c in range(CLASSES):
        prior = prior + jnp.where(label_lane == c, log_prior[:, c : c + 1], 0.0)
    image_lane = lax.broadcasted_iota(jnp.int32, (1, img_dev), 1)

    blocks = []
    for il in range(OWNED):
        noise = jnp.sum(jnp.where(image_lane == OWNED * r + il, precision[...], 0.0), axis=1, keepdims=True)
        scores = noise * mine[il] + prior
        scores = jnp.where(row < PAIRS, scores, -jnp.inf)
        top = jnp.max(jnp.max(scores, axis=1, keepdims=True), axis=0, keepdims=True)
        exponent = jnp.exp(scores - top)
        row_total = jnp.sum(jnp.sum(exponent, axis=1, keepdims=True), axis=0, keepdims=True)
        posterior = exponent / row_total
        lane_sum = jnp.broadcast_to(jnp.sum(posterior, axis=0, keepdims=True), (8, LANES))
        totals = lane_sum + pltpu.roll(lane_sum, n_refs, 1)
        for c in range(CLASSES):
            in_class = jnp.sum(jnp.where(label_lane == c, lane_sum, 0.0), axis=1, keepdims=True)
            totals = jnp.where(lane == n_refs + c, in_class, totals)
        high = totals.astype(jnp.bfloat16).astype(jnp.float32)
        block = jnp.where(row == PAIRS, high, posterior)
        blocks.append(jnp.where(row == PAIRS + 1, totals - high, block))
    post_buf[me] = jnp.concatenate(blocks, axis=0).astype(jnp.bfloat16)

    def post_copy(j):
        other = lax.rem(me + j, n_dev)
        return exchange(
            post_buf.at[me], post_buf.at[me], post_ss.at[j], post_rs.at[j], other // n_ref, lax.rem(other, n_ref)
        )

    def post_start(j, carry):
        post_copy(j).start()
        return carry

    lax.fori_loop(1, n_dev, post_start, 0)

    def post_arrive(j, carry):
        source = lax.rem(me + n_dev - j, n_dev)
        exchange(
            post_buf.at[me], post_buf.at[source], post_ss.at[j], post_rs.at[j], source // n_ref, lax.rem(source, n_ref)
        ).wait_recv()
        return carry

    lax.fori_loop(1, n_dev, post_arrive, 0)

    post_wide[...] = post_buf[...].astype(jnp.float32).reshape(n_images, 8, LANES)
    totals = post_wide[:, PAIRS, :] + post_wide[:, PAIRS + 1, :]
    mass = jnp.broadcast_to(jnp.sum(totals, axis=0, keepdims=True), (LANES, LANES)).T[0:n_refs]
    scale = 1.0 / (mass[:, 0:1] + 1.0)
    first = pl.ds(a * img_dev, img_dev)
    mine = post_wide[first, PAIRS, :] + post_wide[first, PAIRS + 1, :]
    class_post[...] = jnp.concatenate([mine] * (LANES // img_dev), axis=0).T[n_refs : n_refs + CLASSES, 0:img_dev]
    weights = []
    for tp in range(PAIRS):
        both = post_wide[:, tp, :].T
        weights.append(jnp.concatenate([both[0:n_refs], both[n_refs : 2 * n_refs]], axis=1).astype(jnp.bfloat16))
    weights = jnp.concatenate(weights, axis=1)
    turned = rotated[...].reshape(SHIFTS * n_images, 2 * CHUNK)
    piece = lax.rem(r, per) * n_img + a

    target = r // per
    turned_y = target // CORES != y
    middle = y * CORES + lax.rem(target, CORES)

    def out_by_way(j):
        if not TURN_OUT:
            return jnp.bool_(False)
        return turned_y & jnp.logical_not((middle == a) & (j == r))

    def out_copy(h, j):
        return exchange(
            out_send.at[h, j], out_buf.at[h, piece], out_ss.at[h, j], out_rs.at[h, piece], target, j
        )

    def out_hop(h, j):
        slot = core * per + lax.rem(r, per)
        return exchange(
            out_send.at[h, j], out_mid.at[h, slot], out_ss.at[h, j], out_mid_rs.at[h, slot], middle, j
        )

    def out_forward(h, slot):
        from_img = y * CORES + slot // per
        from_ref = per * across + slot % per
        arrived = (slot % per) * n_img + from_img
        return (from_img == a) & (from_ref == r), exchange(
            out_mid.at[h, slot], out_buf.at[h, arrived], out_mid_ss.at[h, slot], out_rs.at[h, arrived], across, r
        )

    for h in range(CHUNK // STRIP):
        real = jnp.dot(weights, turned[:, h * STRIP : (h + 1) * STRIP], preferred_element_type=jnp.float32)
        imag = jnp.dot(
            weights, turned[:, CHUNK + h * STRIP : CHUNK + (h + 1) * STRIP], preferred_element_type=jnp.float32
        )
        real = (real * scale).reshape(n_ref, REF_ROWS, STRIP)
        imag = (imag * scale).reshape(n_ref, REF_ROWS, STRIP)
        out_send[h] = jnp.concatenate([real, imag], axis=1).astype(jnp.bfloat16)

        def out_start(i, carry):
            j = lax.rem(r + i, n_ref)
            here = (a == target) & (j == r)
            by_way = out_by_way(j)

            @pl.when(here)
            def _():
                out_buf[h, piece] = out_send[h, j]

            @pl.when(by_way)
            def _():
                out_hop(h, j).start()

            @pl.when(jnp.logical_not(here | by_way))
            def _():
                out_copy(h, j).start()

            return carry

        lax.fori_loop(0, n_ref, out_start, 0)

    if TURN_OUT:
        for h in range(CHUNK // STRIP):
            for slot in range(per * CORES):
                stays, copy = out_forward(h, slot)

                @pl.when(jnp.logical_not(stays))
                def _():
                    exchange(
                        out_send.at[h, 0], out_mid.at[h, slot], out_ss.at[h, 0], out_mid_rs.at[h, slot], a, 0
                    ).wait_recv()
                    copy.start()

    for h in range(CHUNK // STRIP):
        for q in range(n_ref):
            @pl.when(jnp.logical_not(ref_here(q)))
            def _():
                exchange(
                    out_send.at[h, 0], out_buf.at[h, q], out_ss.at[h, 0], out_rs.at[h, q],
                    q % n_img, per * a + q // n_img,
                ).wait_recv()

            new_refs[:, q * CHUNK + h * STRIP : q * CHUNK + (h + 1) * STRIP] = out_buf[h, q]

    for copy in img_copies + part_copies + own_copies:
        copy.wait_send()

    def post_sent(j, carry):
        post_copy(j).wait_send()
        return carry

    lax.fori_loop(1, n_dev, post_sent, 0)

    def edge_sent(j, carry):
        @pl.when(jnp.logical_not(ref_here(j)))
        def _():
            ref_copy(j).wait_send()

        @pl.when(jnp.logical_not((a == r // per) & (j == r)))
        def _():
            for h in range(CHUNK // STRIP):
                out_copy(h, j).wait_send()

        return carry

    lax.fori_loop(0, n_ref, edge_sent, 0)
    for slot in range(per * CORES):
        if TURN_IN:
            stays, copy = ref_forward(slot)

            @pl.when(jnp.logical_not(stays))
            def _():
                copy.wait_send()

        if TURN_OUT:
            for h in range(CHUNK // STRIP):
                stays, copy = out_forward(h, slot)

                @pl.when(jnp.logical_not(stays))
                def _():
                    copy.wait_send()


def fused(n_img, n_ref, images, references, precision, shifts, labels, log_prior):
    img_dev = images.shape[1]
    n_images = n_img * img_dev
    n_refs = n_ref * REF_ROWS
    n_dev = n_img * n_ref
    vmem = pl.BlockSpec(memory_space=pltpu.VMEM)
    far = pl.BlockSpec(memory_space=pl.ANY)
    low = jnp.bfloat16
    wide = jnp.float32
    strips = CHUNK // STRIP
    per = n_ref // n_img
    parts = (GROUPS, n_img)
    outs = (strips, n_ref)
    counts = ((6,), (n_img,), (n_img,), (n_ref,), (n_ref,), parts, parts)
    counts = counts + ((n_ref,), (n_ref,), (n_dev,), (n_dev,), outs, outs)
    mids = (strips, CORES * per)
    counts = counts + ((CORES * per,), (CORES * per,), mids, mids)
    new_refs, class_rows = pl.pallas_call(
        functools.partial(fused_kernel, n_img, n_ref),
        out_shape=(
            jax.ShapeDtypeStruct((2 * REF_ROWS, references.shape[2]), low),
            jax.ShapeDtypeStruct((CLASSES, img_dev), wide),
        ),
        in_specs=[far] * 6,
        out_specs=(vmem, vmem),
        scratch_shapes=[
            pltpu.VMEM(images.shape, wide),
            pltpu.VMEM(references.shape, wide),
            pltpu.VMEM((1, img_dev), wide),
            pltpu.VMEM((2, SHIFTS), jnp.int32),
            pltpu.VMEM((1, REF_ROWS), jnp.int32),
            pltpu.VMEM((1, CLASSES), wide),
            pltpu.VMEM((n_img, 2, img_dev, CHUNK), low),
            pltpu.VMEM((n_img, 2, img_dev, CHUNK), low),
            pltpu.VMEM((n_ref, 2 * REF_ROWS, CHUNK), low),
            pltpu.VMEM((n_ref, 2 * REF_ROWS, CHUNK), low),
            pltpu.VMEM((SHIFTS, 8, CHUNK), wide),
            pltpu.VMEM((SHIFTS, 8, CHUNK), wide),
            pltpu.VMEM((SHIFTS, n_images, 2 * CHUNK), low),
            pltpu.VMEM((SHIFTS, n_refs, 2 * CHUNK), low),
            pltpu.VMEM((n_refs, LANES), wide),
            pltpu.VMEM((CORES * per, 2 * REF_ROWS, CHUNK), low),
            pltpu.VMEM((strips, CORES * per, 2 * REF_ROWS, STRIP), low),
            pltpu.VMEM((GROUPS, n_img, img_dev, TOGETHER * n_refs), wide),
            pltpu.VMEM((GROUPS, n_img - 1, img_dev, TOGETHER * n_refs), wide),
            pltpu.VMEM((img_dev, 8, LANES), wide),
            pltpu.VMEM((n_ref - 1, OWNED, 8, LANES), wide),
            pltpu.VMEM((n_dev, 16, LANES), low),
            pltpu.VMEM((n_images, 8, LANES), wide),
            pltpu.VMEM((strips, n_ref, 2 * REF_ROWS, STRIP), low),
            pltpu.VMEM((strips, n_ref, 2 * REF_ROWS, STRIP), low),
        ]
        + [pltpu.SemaphoreType.DMA(count) for count in counts],
        compiler_params=pltpu.CompilerParams(
            collective_id=0, has_side_effects=True, vmem_limit_bytes=56 * 1024 * 1024
        ),
        cost_estimate=pl.CostEstimate(flops=800_000_000, bytes_accessed=2_000_000, transcendentals=25_000),
    )(
        images,
        references,
        precision.reshape(1, img_dev),
        shifts.T,
        labels.reshape(1, REF_ROWS),
        log_prior.reshape(1, CLASSES),
    )
    return new_refs.reshape(references.shape).astype(wide), class_rows.T


def local(n_img, n_ref, images, references, precision, shifts, labels, log_prior):
    fits = (
        images.shape[1] == OWNED * n_ref
        and images.shape[1] % 16 == 0
        and references.shape[1] == REF_ROWS
        and 2 * n_ref * REF_ROWS == LANES
        and images.shape[2] == n_img * CHUNK
        and references.shape[2] == n_ref * CHUNK
        and n_ref % n_img == 0
        and n_img == 2 * CORES
    )
    if fits:
        return fused(n_img, n_ref, images, references, precision, shifts, labels, log_prior)
    return gathered(images, references, precision, shifts, labels, log_prior)


def solution(mesh):
    return jax.shard_map(
        functools.partial(local, mesh.shape["img"], mesh.shape["ref"]),
        mesh=mesh,
        in_specs=(P(None, "img", "ref"), P(None, "ref", "img"), P("img"), P(), P("ref"), P()),
        out_specs=(P(None, "ref", "img"), P("img", None)),
        check_vma=False,
    )
```

profile of v0, /device:TPU:0, one launch (start us, length us, event | category | flops | bytes accessed | tf_op | source)
XLA Modules:
  0.0 50.0 jit_solution(8039925042351382097)
XLA Ops:
  0.6 47.0 %shard_map.77 = (bf16[16,8192]{1,0:T(8,128)(2,1)}, f32[4,16]{1,0:T(4,128)}) custom-call(f32[2,16,4096]{2,1,0:T(8,128)} %images_hbm.1, f32[2,8,8192]{2,1,0:T(8,128)} %references_hbm.1, f32[1,16]{1,0:T(1,128)} %bitcast.10, s32[2,12]{1,0:T(2,128)} %bitcast.9, s32[1,8]{1,0:T(1,128)} %bitcast.11, f32[1,4]{1,0:T(1,128)} %bitcast.12), custom_call_target="tpu_custom_call" | custom-call | flops 800000000 | bytes 2000000 | tf_op jit(solution)/shard_map/pallas_call | solution.py:570
  47.6 0.0 copy-start
  47.6 1.8 %bitcast_convert_fusion = f32[2,8,8192]{2,1,0:T(8,128)} fusion(bf16[16,8192]{1,0:T(8,128)(2,1)} %get-tuple-element.4), kind=kLoop, calls=%fused_computation | loop fusion | flops 131072 | bytes 786432 | tf_op jit(solution)/shard_map/convert_element_type | solution.py:618
  49.4 0.0 copy-done
  49.4 0.6 %copy.9 = f32[16,4]{0,1:T(4,128)} copy(f32[16,4]{0,1:T(4,128)S(1)} %bitcast.8) | data formatting | bytes 512
Async XLA Ops:
  47.6 1.8 %copy-start = (f32[4,16]{1,0:T(4,128)S(1)}, f32[4,16]{1,0:T(4,128)}, u32[]{:S(2)}) copy-start(f32[4,16]{1,0:T(4,128)} %get-tuple-element.5) | copy-start | bytes 772
where the time goes:
time: 50.1 us; the launch traced here: 50 us
  Pallas kernels  47 us (94%)
  other arithmetic  1.78 us (4%)
  between operations  0.65 us (1%)
  local copies, waits for them, and re-layouts  0.58 us (1%)
    pallas_call x1, Pallas kernels, fused(): pl.pallas_call(functools.partial(fused_kernel, n_img, n_ref), out_shape=(...  47 us
    convert_element_type x1, other arithmetic, fused(): return (new_refs.reshape(references.shape).astype(wide), class_rows.T)  1.78 us

commit v1 on v0

--- a/solution.py
+++ b/solution.py
@@ -107,8 +107,8 @@
 GROUPS = SHIFTS // TOGETHER
 STRIP = 512
 CORES = 2
-TURN_IN = False
-TURN_OUT = True
+TURN_IN = True
+TURN_OUT = False
 REF_ROWS = 8
 
 
@@ -548,6 +548,15 @@
                 @pl.when(jnp.logical_not(stays))
                 def _():
                     copy.wait_send()
+
+
+def widen_kernel(low, class_rows, new_refs, class_post):
+    for q in range(low.shape[1] // CHUNK):
+        px = slice(q * CHUNK, (q + 1) * CHUNK)
+        block = low[:, px].astype(jnp.float32)
+        new_refs[0, :, px] = block[0:REF_ROWS]
+        new_refs[1, :, px] = block[REF_ROWS : 2 * REF_ROWS]
+    class_post[...] = class_rows[...]
 
 
 def fused(n_img, n_ref, images, references, precision, shifts, labels, log_prior):
@@ -615,7 +624,17 @@
         labels.reshape(1, REF_ROWS),
         log_prior.reshape(1, CLASSES),
     )
-    return new_refs.reshape(references.shape).astype(wide), class_rows.T
+    new_refs, class_rows = pl.pallas_call(
+        widen_kernel,
+        out_shape=(
+            jax.ShapeDtypeStruct(references.shape, wide),
+            jax.ShapeDtypeStruct((CLASSES, img_dev), wide),
+        ),
+        in_specs=[vmem, vmem],
+        out_specs=(vmem, vmem),
+        cost_estimate=pl.CostEstimate(flops=0, bytes_accessed=800_000, transcendentals=0),
+    )(new_refs, class_rows)
+    return new_refs, class_rows.T
 
 
 def local(n_img, n_ref, images, references, precision, shifts, labels, log_prior):

time: 50.1 us -> 44.8 us (0.89)
  the two profiles are of different devices: /device:TPU:0 before, /device:TPU:25 now
where the time goes in v1:
time: 44.8 us; the launch traced here: 44.7 us
  Pallas kernels  44 us (98%)
  between operations  0.64 us (1%)
    pallas_call x1, Pallas kernels, fused(): pl.pallas_call(functools.partial(fused_kernel, n_img, n_ref), out_shape=(...  42.2 us
    pallas_call x1, Pallas kernels, fused(): pl.pallas_call(widen_kernel, out_shape=(jax.ShapeDtypeStruct(references.s...  1.78 us

profile of v1, /device:TPU:25, one launch (start us, length us, event | category | flops | bytes accessed | tf_op | source)
XLA Modules:
  0.0 44.7 jit_solution(2838093962453532966)
XLA Ops:
  0.6 42.2 %shard_map.77 = (bf16[16,8192]{1,0:T(8,128)(2,1)}, f32[4,16]{1,0:T(4,128)}) custom-call(f32[2,16,4096]{2,1,0:T(8,128)} %images_hbm.1, f32[2,8,8192]{2,1,0:T(8,128)} %references_hbm.1, f32[1,16]{1,0:T(1,128)} %bitcast.7, s32[2,12]{1,0:T(2,128)} %bitcast.6, s32[1,8]{1,0:T(1,128)} %bitcast.8, f32[1,4]{1,0:T(1,128)} %bitcast.9), custom_call_target="tpu_custom_call" | custom-call | flops 800000000 | bytes 2000000 | tf_op jit(solution)/shard_map/pallas_call | solution.py:579
  42.9 1.8 %shard_map.78 = (f32[2,8,8192]{2,1,0:T(8,128)}, f32[4,16]{1,0:T(4,128)}) custom-call(bf16[16,8192]{1,0:T(8,128)(2,1)} %get-tuple-element.6.low, f32[4,16]{1,0:T(4,128)} %get-tuple-element.7.class_rows), custom_call_target="tpu_custom_call" | custom-call | bytes 800000 | tf_op jit(solution)/shard_map/pallas_call | solution.py:627
